TPU v7x, 768 devices: a whole 4x8x12 slice. The times are simulated.
768 devices in a mesh: row: 32 (over y, z_lo), col: 24 (over z_hi, x, core).
Axes of the slice: x: 4, y: 8, z: 12 (z_hi: 3, z_lo: 4; z = z_hi * 4 + z_lo), core: 2. Of those that a mesh axis runs over, the one named last changes fastest.
Arguments:
- a_vals: bfloat16 [32, 264, 128, 128], P('row', 'col'), may hold values from -0.0625 to 0.0625
- a_row: int32 [32, 264], P('row', 'col'), may hold values from 0 to 4, as said below
- a_col: int32 [32, 264], P('row', 'col'), may hold values from 0 to 767, as said below
- group_rows: int32 [32], P('row'), may hold values from 1 to 4, 96 in all
- b_panel: bfloat16 [98304, 3072], P('row', 'col'), may hold values from -6 to 6
- c_mask: int32 [128, 24], P('row', 'col'), may hold values 0 or 1
Outputs:
- product: bfloat16 [16384, 3072], P('row', 'col')
Inputs may be any that keep to these rules, and one draw needn't show every extreme that they name: `a_row`: 4 marks an empty slot; every slot from 256 on is empty; slots with equal s // 4 below that name different block rows or are empty. `a_col`: slots with equal s // 4 below 256 name the same block column k, with k // 24 == s // 8.
All inputs are finite; a program needn't handle non-finite values. No bound on the sum of `group_rows` or of `c_mask` on one device may be relied on, other than what follows from the above.
Results may differ from a plain program's by a relative error of at most 0.011.
Values may be sent and summed in bfloat16 or wider, within the bound.
A program may use at most 64 MiB of HBM per device.

v0:
```python
import jax
import jax.numpy as jnp
from jax import lax
from jax.sharding import PartitionSpec as P

BS = 128
RCAP = 4
CAPQ = 2
KB_DEV = 24


def send_back(blocks):
    return lax.all_to_all(blocks, "row", split_axis=0, concat_axis=0, tiled=True)


def per_device(a_vals, a_row, a_col, group_rows, b_panel, c_mask):
    owners = lax.axis_size("row")
    lists = owners * CAPQ
    used = lists * RCAP
    cols_all = lax.all_gather(a_col, "col", axis=1, tiled=True)
    wanted_cols = cols_all[0, :used].reshape(lists, RCAP)[:, 0].reshape(owners, CAPQ)
    wanted_cols = wanted_cols - jnp.arange(owners, dtype=jnp.int32)[:, None] * KB_DEV
    panel_blocks = b_panel.reshape(KB_DEV, BS, BS)
    fetched = send_back(
        panel_blocks[lax.all_to_all(wanted_cols, "row", split_axis=0, concat_axis=0, tiled=True)]
    )
    fetched = fetched.reshape(lists, BS, BS)
    live_count = group_rows[0]
    places = jnp.arange(RCAP, dtype=jnp.int32)
    blocks_all, rows_all = (
        lax.all_gather(a_vals, "col", axis=1, tiled=True),
        lax.all_gather(a_row, "col", axis=1, tiled=True),
    )
    blocks = blocks_all[0, :used].reshape(lists, RCAP, BS, BS)
    slot_rows = rows_all[0, :used].reshape(lists, RCAP)
    onehot = (
        (slot_rows[:, :, None] == places[None, None, :]) & (slot_rows[:, :, None] < live_count)
    ).astype(jnp.bfloat16)
    placed = jnp.einsum("lri,lrab->liab", onehot, blocks, preferred_element_type=jnp.bfloat16)
    full = jnp.einsum("liab,lbn->ian", placed, fetched, preferred_element_type=jnp.float32)
    full = full * c_mask.astype(jnp.float32)[:, 0][:, None, None]
    return full.reshape(RCAP * BS, BS).astype(jnp.bfloat16)


def solution(mesh):
    in_specs = (
        P("row", "col", None, None),
        P("row", "col"),
        P("row", "col"),
        P("row"),
        P("row", "col"),
        P("row", "col"),
    )
    out_specs = P("row", "col")
    return jax.shard_map(
        per_device, mesh=mesh, in_specs=in_specs, out_specs=out_specs, check_vma=False
    )
```

profile of v0, /device:TPU:1, one launch (start us, length us, event | category | flops | bytes accessed | tf_op | source)
XLA Modules:
  0.0 217.6 jit_solution(8781077215635311847)
XLA Ops:
  6.5 0.0 copy-start
  6.5 0.0 all-gather.2.cloned.1.call-start
  6.5 0.7 all-gather.2.cloned.1.call-update
  7.3 1.3 dynamic-slice
  9.2 0.8 bitcast_dynamic-update-slice_fusion
  10.0 0.7 bitcast_dynamic-update-slice_fusion.1
  10.7 85.6 %all-reduce.2 = (s32[264]{0:T(512)S(1)}, s32[264]{0:T(512)S(1)}) all-reduce(s32[264]{0:T(512)S(1)} %bitcast_dynamic-update-slice_fusion, s32[264]{0:T(512)S(1)} %bitcast_dynamic-update-slice_fusion.1), channel_id=1, replica_groups=mesh['row'=32,'col'=24] {'col'}, use_global_device_ids=true, to_apply=%add.1 | all-reduce | flops 528 | bytes 4224
  96.3 0.1 reshape_squeeze.10
  96.4 0.1 slice_reduce_fusion
  96.6 0.1 reshape_squeeze.11
  96.7 0.1 broadcast_subtract_fusion
  96.8 19.8 %all_to_all.14 = s32[32,1,2]{2,1,0:T(1,128)S(1)} all-to-all(s32[32,1,2]{2,1,0:T(1,128)S(1)} %bitcast.41), channel_id=1, replica_groups=mesh['row'=32,'col'=24] {'row'}, dimensions={0} | all-to-all | bytes 512 | tf_op jit(solution)/shard_map/all_to_all | solution.py:25
  116.5 0.1 copy.20
  116.6 0.1 copy.21
  116.7 0.1 reshape.84
  116.8 0.0 copy-done
  116.8 2.1 gather_fusion
  119.0 34.0 %all-to-all-start.1 = ((bf16[32,2,128,128]{3,2,1,0:T(8,128)(2,1)}), bf16[32,2,128,128]{3,2,1,0:T(8,128)(2,1)S(1)}, u32[]{:S(2)}, u32[]{:S(2)}) async-start(bf16[32,2,128,128]{3,2,1,0:T(8,128)(2,1)} %bitcast.12), calls=%async_computation.1 | async-start | bytes 4194304 | tf_op jit(solution)/shard_map/all_to_all | solution.py:13
  153.6 0.1 eq.15
  153.8 0.0 all-gather.2.cloned.1.call-done
  153.8 10.4 %slice.19 = bf16[1,256,128,128]{3,2,1,0:T(8,128)(2,1)} slice(bf16[1,264,128,128]{3,2,1,0:T(8,128)(2,1)} %bitcast.38), slice={[0:1], [0:256], [0:128], [0:128]} | slice | bytes 16777216 | tf_op jit(solution)/shard_map/slice | solution.py:34
  164.2 12.2 %fusion.2 = bf16[64,4,128,128]{3,1,2,0:T(4,128)(2,1)} fusion(bf16[64,4,128,128]{3,2,1,0:T(8,128)(2,1)} %bitcast.37, s32[64,4]{1,0:T(8,128)S(1)} %eq.15, pred[64,4]{1,0:T(8,128)(4,1)S(1)} %broadcast_compare_fusion), kind=kOutput, calls=%fused_computation.3 | convolution fusion | flops 33556480 | bytes 16778496 | tf_op jit(solution)/shard_map/lri,lrab->liab/dot_general | solution.py:39
  176.4 28.0 %all-to-all-done.1 = bf16[32,2,128,128]{3,2,1,0:T(8,128)(2,1)S(1)} async-done(((bf16[32,2,128,128]{3,2,1,0:T(8,128)(2,1)}), bf16[32,2,128,128]{3,2,1,0:T(8,128)(2,1)S(1)}, u32[]{:S(2)}, u32[]{:S(2)}) %all-to-all-start.1) | async-done | bytes 2097184 | tf_op jit(solution)/shard_map/all_to_all | solution.py:13
  204.4 6.4 %fusion.10 = bf16[4,128,128]{2,1,0:T(8,128)(2,1)} fusion(bf16[64,128,128,1]{2,1,0,3:T(8,128)(2,1)S(1)} %bitcast.39, bf16[64,4,128,128]{3,1,2,0:T(4,128)(2,1)} %fusion.2, f32[4]{0:T(128)S(1)} %convert_bitcast_fusion), kind=kOutput, calls=%fused_computation.7 | convolution fusion | flops 1073872896 | bytes 10616848 | tf_op jit(solution)/shard_map/liab,lbn->ian/dot_general | solution.py:40
  (13 shorter events, 0.1 us)
Async XLA Ops:
  6.5 110.3 %copy-start = (bf16[3072,128]{1,0:T(8,128)(2,1)S(1)}, bf16[3072,128]{1,0:T(8,128)(2,1)}, u32[]{:S(2)}) copy-start(bf16[3072,128]{1,0:T(8,128)(2,1)} %param.10) | copy-start | bytes 2359300
  6.5 147.2 %copy-start.1 = (s32[4,1]{0,1:T(1,128)S(1)}, s32[4,1]{0,1:T(1,128)}, u32[]{:S(2)}) copy-start(s32[4,1]{0,1:T(1,128)} %param.11) | copy-start | bytes 52
  6.5 147.3 %all-gather.2.cloned.1.call-start = ((), (), s32[]{:S(2)}) async-start(), calls=%async_computation.2 | async-start | bytes 9011200 | tf_op jit(solution)/shard_map/all_gather | solution.py:31
  119.0 85.4 %all-to-all-start.1 = ((bf16[32,2,128,128]{3,2,1,0:T(8,128)(2,1)}), bf16[32,2,128,128]{3,2,1,0:T(8,128)(2,1)S(1)}, u32[]{:S(2)}, u32[]{:S(2)}) async-start(bf16[32,2,128,128]{3,2,1,0:T(8,128)(2,1)} %bitcast.12), calls=%async_computation.1 | async-start | bytes 4194304 | tf_op jit(solution)/shard_map/all_to_all | solution.py:13
Sparse Core Ops, SparseCore 0:
  11.4 142.0 all-gather.1
where the time goes:
time: 221 us; the launch traced here: 218 us
  blocking collectives  105 us (48%)
  starting transfers between devices  34 us (15%)
  waiting for transfers between devices  28.7 us (13%)
  matrix products  18.6 us (8%)
  local copies, waits for them, and re-layouts  16 us (7%)
  between operations  14.8 us (7%)
    unnamed x1, blocking collectives  85.6 us
    all_to_all x1, starting transfers between devices, send_back(): lax.all_to_all(blocks, 'row', split_axis=0, concat_axis=0, tiled=True)  34 us
    all_to_all x1, waiting for transfers between devices, send_back(): lax.all_to_all(blocks, 'row', split_axis=0, concat_axis=0, tiled=True)  28 us
    all_to_all x1, blocking collectives, per_device(): lax.all_to_all(wanted_cols, 'row', split_axis=0, concat_axis=0, tiled=True)  19.8 us
    dot_general x1, matrix products, per_device(): jnp.einsum('lri,lrab->liab', onehot, blocks, preferred_element_type=jnp.b...  12.2 us
    slice x1, local copies, waits for them, and re-layouts, per_device(): blocks = blocks_all[0, :used].reshape(lists, RCAP, BS, BS)  10.4 us
    dot_general x1, matrix products, per_device(): jnp.einsum('liab,lbn->ian', placed, fetched, preferred_element_type=jnp.f...  6.41 us
  transfers between devices with their start and end apart: 2, of which 1 were waited for; matrix products, arithmetic and copies ran while one was open for 13% of the time, Pallas kernels for 0%

commit v1 on v0

v1 whole, which is shorter than its diff:
```python
import jax
import jax.numpy as jnp
from jax import lax
from jax.experimental import pallas as pl
from jax.experimental.pallas import tpu as pltpu
from jax.sharding import PartitionSpec as P

BS = 128
RCAP = 4
KB_DEV = 24
PER_DEV = 11
USED = 256
N_ROW = 32
N_COL = 24
NY, NZ, NH, NX = 8, 4, 3, 4
LIST8 = 8
ZERO = 64
MESH = pl.DeviceIdType.MESH


def div(a, b):
    return lax.div(jnp.int32(a), jnp.int32(b))


def rem(a, b):
    return lax.rem(jnp.int32(a), jnp.int32(b))


def owners_in(zl, h):
    first = PER_DEV * h + rem(zl + h, NZ)
    last = jnp.minimum(PER_DEV * h + PER_DEV - 1, N_ROW - 1)
    return div(first, NZ), first + 2 * NZ <= last


def kernel(
    a_ref, row_hbm, col_hbm, live_hbm, b_hbm, mask_hbm, out_ref,
    row_ref, col_ref, live_ref, b_ref, mask_ref, l_in, a0, a1, a2, a3, bbuf, bstage, pk, ix1, ix2, sx, rbuf, rs, idxs, ostage, obuf, acc,
    s_i1, r_i1, s_i2, r_i2, l_i2, s_s1, r_s1, s_s2, r_s2, s_x, r_x, s_f, r_f, s_c, r_c,
    s_b, r_b, s_r, r_r, l_r, s_o, r_o,
):
    held = (a0, a1, a2, a3)
    r = lax.axis_index("row")
    c = lax.axis_index("col")
    y, zl = div(r, NZ), rem(r, NZ)
    h, e = div(c, 8), rem(c, 8)
    x, k = div(e, 2), rem(e, 2)
    ca, cb = div(LIST8 * r, PER_DEV), div(LIST8 * r + LIST8 - 1, PER_DEV)
    two = cb != ca
    holds = (c == ca) | (c == cb)
    slot = jnp.where(c == ca, 0, 1)
    o_lo = div(PER_DEV * c, LIST8)
    o_hi = jnp.minimum(div(PER_DEV * c + PER_DEV - 1, LIST8), N_ROW - 1)

    y0, three = owners_in(zl, h)

    def at_h(d):
        return (r, rem(h + d, NH) * 8 + e)

    def at_x(d):
        return (r, h * 8 + rem(x + d, NX) * 2 + k)

    def at_y(d):
        return (rem(y + d, NY) * NZ + zl, c)

    def at_z(z):
        return (y * NZ + z, c)

    other = (r, h * 8 + 2 * x + 1 - k)

    def remote(src, dst, s_sem, r_sem, device):
        return pltpu.make_async_remote_copy(
            src_ref=src, dst_ref=dst, send_sem=s_sem, recv_sem=r_sem,
            device_id=device, device_id_type=MESH,
        )

    loads = [
        pltpu.make_async_copy(src, dst, l_in.at[i])
        for i, (src, dst) in enumerate(
            (
                (row_hbm, row_ref), (col_hbm, col_ref), (live_hbm, live_ref),
                (b_hbm, b_ref), (mask_hbm, mask_ref),
            )
        )
    ]
    for load in loads:
        load.start()

    barrier = pltpu.get_barrier_semaphore()

    def signal(device):
        pl.semaphore_signal(barrier, inc=1, device_id=device, device_id_type=MESH)

    for d in (1, 2):
        signal(at_h(d))
    for d in (1, 3):
        signal(at_x(d))
    signal(other)
    for d in range(1, NY):
        signal(at_y(d))
    for d in range(1, NZ):
        signal(at_z(rem(zl + d, NZ)))

    def greet_s1(i, _):
        g, t = rem(i, NZ), div(i, NZ)
        o = (y0 + t) * NZ + zl
        cs = div(LIST8 * o + e, PER_DEV)
        ok = (t < 2) | three

        @pl.when(ok & ((g != zl) | (cs != c)))
        def _():
            signal((y * NZ + g, cs))

        return 0

    lax.fori_loop(0, 12, greet_s1, 0)

    @pl.when(c != ca)
    def _():
        signal((r, ca))

    @pl.when(two & (c != cb))
    def _():
        signal((r, cb))

    @pl.when(holds)
    def _():
        def greet(i, _):
            signal((rem(r + i, N_ROW), c))
            return 0

        lax.fori_loop(1, N_ROW, greet, 0)

    def is_self(j):
        s = PER_DEV * c + j
        return (rem(div(s, LIST8), NZ) == zl) & (rem(s, LIST8) == e)

    for load in loads[:3]:
        load.wait()
    rows = row_ref[...]
    rows = jnp.where(rows < live_ref[0], rows, RCAP)
    pk[...] = jnp.zeros_like(pk)
    pk[:, 0:PER_DEV] = col_ref[...] * 8 + rows
    for n in range(4):
        held[n][ZERO] = jnp.zeros((BS, BS), jnp.bfloat16)

    expect = jnp.int32(15)
    for j in range(PER_DEV):
        s = PER_DEV * c + j
        expect = expect + jnp.where((s < USED) & jnp.logical_not(is_self(j)), 1, 0)
    for t in range(3):
        expect = expect + jnp.where((o_lo + t <= o_hi) & (o_lo + t != r), 1, 0)
    expect = expect + jnp.where(holds, N_COL - 1, 0)
    pl.semaphore_wait(barrier, expect)

    def i1(t):
        o = o_lo + t
        return (
            (o <= o_hi) & (o != r),
            (o <= o_hi) & (o == r),
            remote(pk, ix1.at[r], s_i1.at[t], r_i1.at[r], (o, c)),
            pltpu.make_async_copy(pk, ix1.at[r], r_i1.at[r]),
        )

    for t in range(3):
        away, here, far, near = i1(t)
        pl.when(away)(far.start)
        pl.when(here)(near.start)

    def send_s1(n):
        zd = rem(zl + 3 - n, NZ)

        def one(j, _):
            s = PER_DEV * c + j
            e2, y2 = rem(s, LIST8), div(s, 4 * LIST8)
            ok = (s < USED) & (rem(div(s, LIST8), NZ) == zd)
            src, dst, sem = a_ref.at[j], held[n].at[e2 * 8 + y2], r_s1.at[n, y2]
            if n == 3:

                @pl.when(ok & (e2 == e))
                def _():
                    pltpu.make_async_copy(src, dst, sem).start()

                ok = ok & (e2 != e)

            @pl.when(ok)
            def _():
                remote(src, dst, s_s1.at[j], sem, (y * NZ + zd, h * 8 + e2)).start()

            return 0

        lax.fori_loop(0, PER_DEV, one, 0)

    for n in range(4):
        send_s1(n)

    def i2(cc):
        return remote(ix1, ix2.at[slot], s_i2.at[cc], r_i2.at[slot], (r, cc))

    @pl.when(holds)
    def _():
        def take(i, _):
            remote(pk, ix1.at[i], s_i1.at[0], r_i1.at[i], other).wait_recv()
            return 0

        lax.fori_loop(0, N_ROW, take, 0)
        pltpu.make_async_copy(ix1, ix2.at[slot], r_i2.at[slot]).start()

        def give(i, _):
            i2(rem(c + i, N_COL)).start()
            return 0

        lax.fori_loop(1, N_COL, give, 0)

    def s2(n, d, part):
        src = held[n].at[pl.ds(e * 8 + y0 + 2 * part, 2 - part)]
        return remote(src, src, s_s2.at[n, d - 1, part], r_s2.at[n, d - 1, part], at_h(d))

    def take_s1(n, t):
        dst = held[n].at[e * 8 + y0 + t]
        remote(dst, dst, s_s1.at[0], r_s1.at[n, y0 + t], other).wait_recv()

    def send_s2(n):
        take_s1(n, 0)
        take_s1(n, 1)
        for d in (1, 2):
            s2(n, d, 0).start()

        @pl.when(three)
        def _():
            take_s1(n, 2)
            for d in (1, 2):
                s2(n, d, 1).start()

    send_s2(0)
    send_s2(1)

    def wait_i2(i):
        remote(ix1, ix2.at[i], s_i2.at[0], r_i2.at[i], other).wait_recv()
        pltpu.make_async_copy(ix2.at[i], sx.at[i], l_i2.at[i]).start()

    wait_i2(0)
    pl.when(two)(lambda: wait_i2(1))
    pltpu.make_async_copy(ix2.at[0], sx.at[0], l_i2.at[0]).wait()
    pl.when(two)(pltpu.make_async_copy(ix2.at[1], sx.at[1], l_i2.at[1]).wait)

    def b_copy(n, d):
        return remote(bstage.at[n, d], bbuf.at[n, y], s_b.at[n, d], r_b.at[n, d], at_y(d))

    def place(o, t):
        s = LIST8 * o + t
        cs = div(s, PER_DEV)
        return jnp.where(cs == div(LIST8 * o, PER_DEV), 0, 1), s - PER_DEV * cs

    def chosen(rr, q):
        which, lane = place(r, RCAP * q)
        return jnp.clip((sx[which, rr, 0, lane] >> 3) - KB_DEV * r, 0, KB_DEV - 1)

    def send_b(n):
        g = rem(zl + 1 + n, NZ)

        def one(i, _):
            d = 1 + rem(3 * i + 3, 7)
            for q in range(2):
                bstage[n, d, q] = b_ref[chosen(rem(y + d, NY) * NZ + g, q)]
            b_copy(n, d).start()
            return 0

        lax.fori_loop(0, NY - 1, one, 0)
        for q in range(2):
            bbuf[n, y, q] = b_ref[chosen(r - zl + g, q)]

    def sent_b(n):
        def one(d, _):
            b_copy(n, d).wait_send()
            return 0

        lax.fori_loop(1, NY, one, 0)

    def r_copy(d, i):
        src = ix2.at[i, pl.ds(rem(y + d, NY) * NZ, NZ)]
        return remote(src, rbuf.at[y, i], s_r.at[d, i], r_r.at[d, i], at_y(d))

    def r_own(i):
        return pltpu.make_async_copy(ix2.at[i, pl.ds(y * NZ, NZ)], rbuf.at[y, i], r_r.at[0, i])

    def send_r():
        def one(d, _):
            r_copy(d, 0).start()
            pl.when(two)(lambda: r_copy(d, 1).start())
            return 0

        lax.fori_loop(1, NY, one, 0)
        r_own(0).start()
        pl.when(two)(lambda: r_own(1).start())

    loads[3].wait()
    send_b(0)
    send_r()
    send_b(1)
    send_b(2)

    def chunk(n, ec, lo=0, size=8):
        return held[n].at[pl.ds(ec * 8 + lo, size)]

    e_of = [rem(x + d, NX) * 2 + k for d in range(NX)]

    def x_copy(n, way):
        src = chunk(n, e)
        return remote(src, src, s_x.at[n, way], r_x.at[n, way], at_x((1, 3)[way]))

    def f_copy(n, way):
        src = chunk(n, e_of[(3, 1)[way]], 4 * way, 4)
        return remote(src, src, s_f.at[n, way], r_f.at[n, way], at_x((1, 3)[way]))

    def c_copy(n, d):
        src = chunk(n, e_of[d])
        return remote(src, src, s_c.at[n, d], r_c.at[n, d], other)

    def landed(ref, sem):
        remote(ref, ref, s_c.at[0, 0], sem, other).wait_recv()

    def own_chunk(n):
        for d in (1, 2):
            ys, three_s = owners_in(zl, rem(h + NH - d, NH))
            at = e * 8 + ys
            landed(held[n].at[pl.ds(at, 2)], r_s2.at[n, d - 1, 0])

            @pl.when(three_s)
            def _(at=at, d=d):
                landed(held[n].at[pl.ds(at + 2, 1)], r_s2.at[n, d - 1, 1])

        x_copy(n, 0).start()
        x_copy(n, 1).start()
        c_copy(n, 0).start()

    def near_chunks(n):
        for way in range(2):
            landed(chunk(n, e_of[(3, 1)[way]]), r_x.at[n, way])
            f_copy(n, way).start()
            c_copy(n, (3, 1)[way]).start()

    def far_chunk(n):
        for way in range(2):
            landed(chunk(n, e_of[2], 4 * way, 4), r_f.at[n, way])
        c_copy(n, 2).start()

    def rows_arrive():
        def wait_r(d, _):
            ys = rem(y + NY - d, NY)
            o = ys * NZ + zl
            both = div(LIST8 * o, PER_DEV) != div(LIST8 * o + LIST8 - 1, PER_DEV)
            landed(rbuf.at[ys, 0], r_r.at[d, 0])
            pltpu.make_async_copy(rbuf.at[ys, 0], rs.at[ys, 0], l_r.at[d, 0]).start()

            @pl.when(both)
            def _():
                landed(rbuf.at[ys, 1], r_r.at[d, 1])
                pltpu.make_async_copy(rbuf.at[ys, 1], rs.at[ys, 1], l_r.at[d, 1]).start()

            return 0

        lax.fori_loop(0, NY, wait_r, 0)

        def wait_l(d, _):
            ys = rem(y + NY - d, NY)
            o = ys * NZ + zl
            both = div(LIST8 * o, PER_DEV) != div(LIST8 * o + LIST8 - 1, PER_DEV)
            pltpu.make_async_copy(rbuf.at[ys, 0], rs.at[ys, 0], l_r.at[d, 0]).wait()
            pl.when(both)(pltpu.make_async_copy(rbuf.at[ys, 1], rs.at[ys, 1], l_r.at[d, 1]).wait)
            return 0

        lax.fori_loop(0, NY, wait_l, 0)

        def invert(i, _):
            ys, g = div(i, NZ), rem(i, NZ)
            o = ys * NZ + zl
            found = [jnp.int32(ZERO)] * LIST8
            for t in range(LIST8):
                which, lane = place(o, t)
                row = rs[ys, which, g, 0, lane] & 7
                for p in range(RCAP):
                    at = (t // RCAP) * RCAP + p
                    found[at] = jnp.where(row == p, t * 8 + ys, found[at])
            for at in range(LIST8):
                idxs[i * LIST8 + at] = found[at]
            return 0

        lax.fori_loop(0, NY * NZ, invert, 0)

    def multiply(n):
        g = rem(zl + 1 + n, NZ)
        for d in range(NX):
            landed(chunk(n, rem(x + d, NX) * 2 + 1 - k), r_c.at[n, d])

        def wait_b(d, _):
            landed(bbuf.at[n, rem(y + NY - d, NY)], r_b.at[n, d])
            return 0

        lax.fori_loop(1, NY, wait_b, 0)
        acc[...] = jnp.zeros_like(acc)

        def step(ys, _):
            at = (ys * NZ + g) * LIST8
            panel = bbuf[n, ys].reshape(2 * BS, BS)
            left = jnp.concatenate(
                [
                    jnp.concatenate([held[n][idxs[at + p]], held[n][idxs[at + RCAP + p]]], axis=1)
                    for p in range(RCAP)
                ],
                axis=0,
            )
            acc[...] += jnp.dot(left, panel, preferred_element_type=jnp.float32)
            return 0

        lax.fori_loop(0, NY, step, 0)

    def o_copy(n):
        return remote(ostage.at[n], obuf.at[n], s_o.at[n], r_o.at[n], at_z(rem(zl + 1 + n, NZ)))

    def hand_over(n):
        multiply(n)
        ostage[n] = acc[...].astype(jnp.bfloat16)
        o_copy(n).start()

    own_chunk(0)
    send_s2(2)
    rows_arrive()
    own_chunk(1)
    send_s2(3)
    near_chunks(0)
    own_chunk(2)
    far_chunk(0)
    near_chunks(1)
    sent_b(0)
    send_b(3)
    own_chunk(3)
    far_chunk(1)
    hand_over(0)
    near_chunks(2)
    hand_over(1)
    far_chunk(2)
    near_chunks(3)
    hand_over(2)
    far_chunk(3)
    loads[4].wait()
    multiply(3)
    for n in range(3):
        landed(obuf.at[n], r_o.at[n])
    for p in range(RCAP):
        at = pl.ds(p * BS, BS)
        total = acc[at, :]
        for n in range(3):
            total = total + obuf[n, at, :].astype(jnp.float32)
        out_ref[at, :] = (total * mask_ref[p, 0].astype(jnp.float32)).astype(jnp.bfloat16)

    for t in range(3):
        away, _, far, _ = i1(t)
        pl.when(away)(far.wait_send)

    def sent_s1(j, _):
        s = PER_DEV * c + j

        @pl.when((s < USED) & jnp.logical_not(is_self(j)))
        def _():
            remote(a_ref.at[j], a0.at[0], s_s1.at[j], r_s1.at[0, 0], other).wait_send()

        return 0

    lax.fori_loop(0, PER_DEV, sent_s1, 0)

    @pl.when(holds)
    def _():
        def sent(i, _):
            i2(rem(c + i, N_COL)).wait_send()
            return 0

        lax.fori_loop(1, N_COL, sent, 0)

    def sent_y(d, _):
        for n in range(1, 4):
            b_copy(n, d).wait_send()
        r_copy(d, 0).wait_send()
        pl.when(two)(lambda: r_copy(d, 1).wait_send())
        return 0

    lax.fori_loop(1, NY, sent_y, 0)
    for n in range(4):
        for d in (1, 2):
            s2(n, d, 0).wait_send()
            pl.when(three)(lambda n=n, d=d: s2(n, d, 1).wait_send())
        for way in range(2):
            x_copy(n, way).wait_send()
            f_copy(n, way).wait_send()
        for d in range(NX):
            c_copy(n, d).wait_send()
        if n < 3:
            o_copy(n).wait_send()


def per_device(a_vals, a_row, a_col, group_rows, b_panel, c_mask):
    vmem, smem, dma = pltpu.VMEM, pltpu.SMEM, pltpu.SemaphoreType.DMA
    block = (BS, BS)
    bf16, i32 = jnp.bfloat16, jnp.int32
    return pl.pallas_call(
        kernel,
        out_shape=jax.ShapeDtypeStruct((RCAP * BS, BS), bf16),
        in_specs=[pl.BlockSpec(memory_space=pl.ANY)] * 6,
        out_specs=pl.BlockSpec(memory_space=vmem),
        scratch_shapes=[
            vmem((1, PER_DEV), i32),
            vmem((1, PER_DEV), i32),
            smem((1,), i32),
            vmem((KB_DEV,) + block, bf16),
            smem((RCAP, 1), i32),
            dma((5,)),
            *[vmem((ZERO + 1,) + block, bf16)] * 4,
            vmem((4, NY, 2) + block, bf16),
            vmem((4, NY, 2) + block, bf16),
            vmem((1, 128), i32),
            vmem((N_ROW, 1, 128), i32),
            vmem((2, N_ROW, 1, 128), i32),
            smem((2, N_ROW, 1, 128), i32),
            vmem((NY, 2, NZ, 1, 128), i32),
            smem((NY, 2, NZ, 1, 128), i32),
            smem((NY * NZ * LIST8,), i32),
            vmem((3, RCAP * BS, BS), bf16),
            vmem((3, RCAP * BS, BS), bf16),
            vmem((RCAP * BS, BS), jnp.float32),
            dma((3,)), dma((N_ROW,)),
            dma((N_COL,)), dma((2,)), dma((2,)),
            dma((PER_DEV,)), dma((4, NY)),
            dma((4, 2, 2)), dma((4, 2, 2)),
            dma((4, 2)), dma((4, 2)),
            dma((4, 2)), dma((4, 2)),
            dma((4, NX)), dma((4, NX)),
            dma((4, NY)), dma((4, NY)),
            dma((NY, 2)), dma((NY, 2)), dma((NY, 2)),
            dma((3,)), dma((3,)),
        ],
        compiler_params=pltpu.CompilerParams(
            collective_id=0, has_side_effects=True, vmem_limit_bytes=40 << 20
        ),
        cost_estimate=pl.CostEstimate(flops=2 * 256 * BS**3, bytes_accessed=2 << 20, transcendentals=0),
    )(
        a_vals.reshape((PER_DEV,) + block),
        a_row,
        a_col,
        group_rows,
        b_panel.reshape((KB_DEV,) + block),
        c_mask,
    )


def solution(mesh):
    in_specs = (
        P("row", "col", None, None),
        P("row", "col"),
        P("row", "col"),
        P("row"),
        P("row", "col"),
        P("row", "col"),
    )
    return jax.shard_map(
        per_device, mesh=mesh, in_specs=in_specs, out_specs=P("row", "col"), check_vma=False
    )
```

time: 221 us -> 113 us (0.51); the launches traced: 218 us -> 113 us
  Pallas kernels: 0 us -> 108 us
  blocking collectives: 105 us -> 0 us
  starting transfers between devices: 34 us -> 0 us
  waiting for transfers between devices: 28.7 us -> 0 us
  matrix products: 18.6 us -> 0 us
  between operations: 14.8 us -> 0.67 us
  local copies, waits for them, and re-layouts: 16 us -> 4.09 us
    pallas_call x0 -> x1, Pallas kernels: none -> 108 us  [per_device(): pl.pallas_call(kernel, out_shape=jax.ShapeDtypeStruct((RCAP * BS, BS), bf...]
    unnamed x1 -> x0, blocking collectives: 85.6 us -> none
    all_to_all x1 -> x0, starting transfers between devices: 34 us -> none  [send_back(): lax.all_to_all(blocks, 'row', split_axis=0, concat_axis=0, tiled=True)]
    all_to_all x1 -> x0, waiting for transfers between devices: 28 us -> none  [send_back(): lax.all_to_all(blocks, 'row', split_axis=0, concat_axis=0, tiled=True)]
    all_to_all x1 -> x0, blocking collectives: 19.8 us -> none  [per_device(): lax.all_to_all(wanted_cols, 'row', split_axis=0, concat_axis=0, tiled=True)]
    dot_general x2 -> x0, matrix products: 18.6 us -> none  [the longest x1 12.2 us: per_device(): jnp.einsum('lri,lrab->liab', onehot, blocks, preferred_element_type=jnp.b...]
    slice x4 -> x0, local copies, waits for them, and re-layouts: 10.5 us -> none  [the longest x1 10.4 us: per_device(): blocks = blocks_all[0, :used].reshape(lists, RCAP, BS, BS)]
  transfers between devices with their start and end apart: 2 -> 0, of which waited for: 1 -> 0; matrix products, arithmetic and copies ran while one was open for 13% -> 0% of each run, Pallas kernels for 0% -> 0%
where the time goes in v1:
time: 113 us
  Pallas kernels  108 us (96%)
  local copies, waits for them, and re-layouts  4.09 us (4%)
    pallas_call x1, Pallas kernels, per_device(): pl.pallas_call(kernel, out_shape=jax.ShapeDtypeStruct((RCAP * BS, BS), bf...  108 us
    unnamed x12, local copies, waits for them, and re-layouts  4.09 us

profile of v1, /device:TPU:1, one launch (start us, length us, event | category | flops | bytes accessed | tf_op | source)
XLA Modules:
  0.0 113.0 jit_solution(13483426897821786009)
XLA Ops:
  0.7 0.0 copy-start.4
  0.7 0.6 copy-done.4
  1.3 0.0 copy-start.2
  1.3 0.0 copy-start.3
  1.3 0.1 copy.7.mask_hbm
  1.4 0.6 copy-done.2
  2.0 0.0 copy-done.3
  2.0 0.0 copy-start
  2.0 1.1 %copy-done = bf16[3072,128]{1,0:T(8,128)(2,1)S(1)} copy-done((bf16[3072,128]{1,0:T(8,128)(2,1)S(1)}, bf16[3072,128]{1,0:T(8,128)(2,1)}, u32[]{:S(2)}) %copy-start) | copy-done | bytes 786456
  3.1 0.0 copy-start.1
  3.1 1.0 copy-done.1
  4.1 108.3 %shard_map.64 = bf16[512,128]{1,0:T(8,128)(2,1)S(1)} custom-call(bf16[11,128,128]{2,1,0:T(8,128)(2,1)S(1)} %bitcast.3, s32[1,11]{1,0:T(1,128)S(1)} %copy-done.2, s32[1,11]{1,0:T(1,128)S(1)} %copy-done.3, s32[1]{0:T(128)S(6)} %copy.9.live_hbm, bf16[24,128,128]{2,1,0:T(8,128)(2,1)S(1)} %bitcast.2, s32[4,1]{1,0:T(4,128)S(1)} %copy.7.mask_hbm), custom_call_target="tpu_custom_call" | custom-call | flops 1073741824 | bytes 2097152 | tf_op jit(solution)/shard_map/pallas_call | solution.py:504
  112.4 0.7 copy.10
Async XLA Ops:
  0.7 0.7 copy-start.4
  1.3 0.7 copy-start.2
  1.3 0.7 copy-start.3
  2.0 1.1 %copy-start = (bf16[3072,128]{1,0:T(8,128)(2,1)S(1)}, bf16[3072,128]{1,0:T(8,128)(2,1)}, u32[]{:S(2)}) copy-start(bf16[3072,128]{1,0:T(8,128)(2,1)} %param.10) | copy-start | bytes 2359300
  3.1 1.0 copy-start.1

commit v2 on v1

--- a/solution.py
+++ b/solution.py
@@ -51,7 +51,8 @@
     o_lo = div(PER_DEV * c, LIST8)
     o_hi = jnp.minimum(div(PER_DEV * c + PER_DEV - 1, LIST8), N_ROW - 1)
 
-    y0, three = owners_in(zl, h)
+    runs = [owners_in(zl, rem(h + d, NH)) for d in range(NH)]
+    y0, three = runs[0]
 
     def at_h(d):
         return (r, rem(h + d, NH) * 8 + e)
@@ -190,8 +191,8 @@
 
         lax.fori_loop(0, PER_DEV, one, 0)
 
-    for n in range(4):
-        send_s1(n)
+    send_s1(0)
+    send_s1(1)
 
     def i2(cc):
         return remote(ix1, ix2.at[slot], s_i2.at[cc], r_i2.at[slot], (r, cc))
@@ -231,8 +232,69 @@
             for d in (1, 2):
                 s2(n, d, 1).start()
 
+    def chunk(n, ec, lo=0, size=8):
+        return held[n].at[pl.ds(ec * 8 + lo, size)]
+
+    e_of = [rem(x + d, NX) * 2 + k for d in range(NX)]
+
+    def run(n, ec, d, part):
+        return held[n].at[pl.ds(ec * 8 + runs[d][0] + 2 * part, 2 - part)]
+
+    def x_copy(n, way, d, part):
+        src = run(n, e, d, part)
+        return remote(src, src, s_x.at[n, way, d, part], r_x.at[n, way, d, part], at_x((1, 3)[way]))
+
+    def send_x(n, d):
+        x_copy(n, 0, d, 0).start()
+        x_copy(n, 1, d, 0).start()
+
+        @pl.when(runs[d][1])
+        def _():
+            x_copy(n, 0, d, 1).start()
+            x_copy(n, 1, d, 1).start()
+
+    def f_copy(n, way):
+        src = chunk(n, e_of[(3, 1)[way]], 4 * way, 4)
+        return remote(src, src, s_f.at[n, way], r_f.at[n, way], at_x((1, 3)[way]))
+
+    def c_copy(n, d):
+        src = chunk(n, e_of[d])
+        return remote(src, src, s_c.at[n, d], r_c.at[n, d], other)
+
+    def landed(ref, sem):
+        remote(ref, ref, s_c.at[0, 0], sem, other).wait_recv()
+
+    def own_chunk(n):
+        for d in (1, 2):
+            landed(run(n, e, NH - d, 0), r_s2.at[n, d - 1, 0])
+
+            @pl.when(runs[NH - d][1])
+            def _(d=d):
+                landed(run(n, e, NH - d, 1), r_s2.at[n, d - 1, 1])
+
+            send_x(n, NH - d)
+        c_copy(n, 0).start()
+
+    def near_chunks(n):
+        for way in range(2):
+            ec = e_of[(3, 1)[way]]
+            for d in range(NH):
+                landed(run(n, ec, d, 0), r_x.at[n, way, d, 0])
+
+                @pl.when(runs[d][1])
+                def _(way=way, ec=ec, d=d):
+                    landed(run(n, ec, d, 1), r_x.at[n, way, d, 1])
+
+            f_copy(n, way).start()
+            c_copy(n, (3, 1)[way]).start()
+
+    def far_chunk(n):
+        for way in range(2):
+            landed(chunk(n, e_of[2], 4 * way, 4), r_f.at[n, way])
+        c_copy(n, 2).start()
+
     send_s2(0)
-    send_s2(1)
+    send_x(0, 0)
 
     def wait_i2(i):
         remote(ix1, ix2.at[i], s_i2.at[0], r_i2.at[i], other).wait_recv()
@@ -294,55 +356,14 @@
         pl.when(two)(lambda: r_own(1).start())
 
     loads[3].wait()
+    send_s1(2)
+    send_s1(3)
     send_b(0)
+    send_s2(1)
+    send_x(1, 0)
     send_r()
     send_b(1)
     send_b(2)
-
-    def chunk(n, ec, lo=0, size=8):
-        return held[n].at[pl.ds(ec * 8 + lo, size)]
-
-    e_of = [rem(x + d, NX) * 2 + k for d in range(NX)]
-
-    def x_copy(n, way):
-        src = chunk(n, e)
-        return remote(src, src, s_x.at[n, way], r_x.at[n, way], at_x((1, 3)[way]))
-
-    def f_copy(n, way):
-        src = chunk(n, e_of[(3, 1)[way]], 4 * way, 4)
-        return remote(src, src, s_f.at[n, way], r_f.at[n, way], at_x((1, 3)[way]))
-
-    def c_copy(n, d):
-        src = chunk(n, e_of[d])
-        return remote(src, src, s_c.at[n, d], r_c.at[n, d], other)
-
-    def landed(ref, sem):
-        remote(ref, ref, s_c.at[0, 0], sem, other).wait_recv()
-
-    def own_chunk(n):
-        for d in (1, 2):
-            ys, three_s = owners_in(zl, rem(h + NH - d, NH))
-            at = e * 8 + ys
-            landed(held[n].at[pl.ds(at, 2)], r_s2.at[n, d - 1, 0])
-
-            @pl.when(three_s)
-            def _(at=at, d=d):
-                landed(held[n].at[pl.ds(at + 2, 1)], r_s2.at[n, d - 1, 1])
-
-        x_copy(n, 0).start()
-        x_copy(n, 1).start()
-        c_copy(n, 0).start()
-
-    def near_chunks(n):
-        for way in range(2):
-            landed(chunk(n, e_of[(3, 1)[way]]), r_x.at[n, way])
-            f_copy(n, way).start()
-            c_copy(n, (3, 1)[way]).start()
-
-    def far_chunk(n):
-        for way in range(2):
-            landed(chunk(n, e_of[2], 4 * way, 4), r_f.at[n, way])
-        c_copy(n, 2).start()
 
     def rows_arrive():
         def wait_r(d, _):
@@ -424,10 +445,12 @@
 
     own_chunk(0)
     send_s2(2)
-    rows_arrive()
+    send_x(2, 0)
     own_chunk(1)
     send_s2(3)
+    send_x(3, 0)
     near_chunks(0)
+    rows_arrive()
     own_chunk(2)
     far_chunk(0)
     near_chunks(1)
@@ -489,7 +512,9 @@
             s2(n, d, 0).wait_send()
             pl.when(three)(lambda n=n, d=d: s2(n, d, 1).wait_send())
         for way in range(2):
-            x_copy(n, way).wait_send()
+            for d in range(NH):
+                x_copy(n, way, d, 0).wait_send()
+                pl.when(runs[d][1])(lambda n=n, way=way, d=d: x_copy(n, way, d, 1).wait_send())
             f_copy(n, way).wait_send()
         for d in range(NX):
             c_copy(n, d).wait_send()
@@ -530,7 +555,7 @@
             dma((N_COL,)), dma((2,)), dma((2,)),
             dma((PER_DEV,)), dma((4, NY)),
             dma((4, 2, 2)), dma((4, 2, 2)),
-            dma((4, 2)), dma((4, 2)),
+            dma((4, 2, NH, 2)), dma((4, 2, NH, 2)),
             dma((4, 2)), dma((4, 2)),
             dma((4, NX)), dma((4, NX)),
             dma((4, NY)), dma((4, NY)),

time: 113 us -> 105 us (0.929)
  the two profiles are of different devices: /device:TPU:1 before, /device:TPU:9 now
where the time goes in v2:
time: 105 us
  Pallas kernels  99.8 us (95%)
  local copies, waits for them, and re-layouts  4.09 us (4%)
    pallas_call x1, Pallas kernels, per_device(): pl.pallas_call(kernel, out_shape=jax.ShapeDtypeStruct((RCAP * BS, BS), bf...  99.8 us
    unnamed x12, local copies, waits for them, and re-layouts  4.09 us

profile of v2, /device:TPU:9, one launch (start us, length us, event | category | flops | bytes accessed | tf_op | source)
XLA Modules:
  0.0 104.5 jit_solution(1105385301851516058)
XLA Ops:
  0.7 0.0 copy-start.4
  0.7 0.6 copy-done.4
  1.3 0.0 copy-start.2
  1.3 0.0 copy-start.3
  1.3 0.1 copy.7.mask_hbm
  1.4 0.6 copy-done.2
  2.0 0.0 copy-done.3
  2.0 0.0 copy-start
  2.0 1.1 %copy-done = bf16[3072,128]{1,0:T(8,128)(2,1)S(1)} copy-done((bf16[3072,128]{1,0:T(8,128)(2,1)S(1)}, bf16[3072,128]{1,0:T(8,128)(2,1)}, u32[]{:S(2)}) %copy-start) | copy-done | bytes 786456
  3.1 0.0 copy-start.1
  3.1 1.0 copy-done.1
  4.1 99.8 %shard_map.64 = bf16[512,128]{1,0:T(8,128)(2,1)S(1)} custom-call(bf16[11,128,128]{2,1,0:T(8,128)(2,1)S(1)} %bitcast.3, s32[1,11]{1,0:T(1,128)S(1)} %copy-done.2, s32[1,11]{1,0:T(1,128)S(1)} %copy-done.3, s32[1]{0:T(128)S(6)} %copy.9.live_hbm, bf16[24,128,128]{2,1,0:T(8,128)(2,1)S(1)} %bitcast.2, s32[4,1]{1,0:T(4,128)S(1)} %copy.7.mask_hbm), custom_call_target="tpu_custom_call" | custom-call | flops 1073741824 | bytes 2097152 | tf_op jit(solution)/shard_map/pallas_call | solution.py:529
  103.9 0.7 copy.10
Async XLA Ops:
  0.7 0.7 copy-start.4
  1.3 0.7 copy-start.2
  1.3 0.7 copy-start.3
  2.0 1.1 %copy-start = (bf16[3072,128]{1,0:T(8,128)(2,1)S(1)}, bf16[3072,128]{1,0:T(8,128)(2,1)}, u32[]{:S(2)}) copy-start(bf16[3072,128]{1,0:T(8,128)(2,1)} %param.10) | copy-start | bytes 2359300
  3.1 1.0 copy-start.1

commit v3 on v2

--- a/solution.py
+++ b/solution.py
@@ -295,6 +295,10 @@
 
     send_s2(0)
     send_x(0, 0)
+    send_s2(1)
+    send_x(1, 0)
+    send_s1(2)
+    send_s1(3)
 
     def wait_i2(i):
         remote(ix1, ix2.at[i], s_i2.at[0], r_i2.at[i], other).wait_recv()
@@ -356,11 +360,7 @@
         pl.when(two)(lambda: r_own(1).start())
 
     loads[3].wait()
-    send_s1(2)
-    send_s1(3)
     send_b(0)
-    send_s2(1)
-    send_x(1, 0)
     send_r()
     send_b(1)
     send_b(2)
@@ -563,7 +563,7 @@
             dma((3,)), dma((3,)),
         ],
         compiler_params=pltpu.CompilerParams(
-            collective_id=0, has_side_effects=True, vmem_limit_bytes=40 << 20
+            collective_id=0, has_side_effects=True, vmem_limit_bytes=60 << 20
         ),
         cost_estimate=pl.CostEstimate(flops=2 * 256 * BS**3, bytes_accessed=2 << 20, transcendentals=0),
     )(

time: 105 us -> 102 us (0.971)
  the two profiles are of different devices: /device:TPU:9 before, /device:TPU:1 now
where the time goes in v3:
time: 102 us
  Pallas kernels  98.7 us (97%)
  local copies, waits for them, and re-layouts  2.88 us (3%)
    pallas_call x1, Pallas kernels, per_device(): pl.pallas_call(kernel, out_shape=jax.ShapeDtypeStruct((RCAP * BS, BS), bf...  98.7 us
    unnamed x4, local copies, waits for them, and re-layouts  2.88 us

profile of v3, /device:TPU:1, one launch (start us, length us, event | category | flops | bytes accessed | tf_op | source)
XLA Modules:
  0.0 102.2 jit_solution(2851144394013895890)
XLA Ops:
  0.7 0.0 copy-start
  0.7 0.6 copy-done
  1.3 0.7 copy.7.mask_hbm
  2.0 98.7 %shard_map.64 = bf16[512,128]{1,0:T(8,128)(2,1)} custom-call(bf16[11,128,128]{2,1,0:T(8,128)(2,1)} %bitcast.3, s32[1,11]{1,0:T(1,128)} %row_hbm.1, s32[1,11]{1,0:T(1,128)} %col_hbm.1, s32[1]{0:T(128)S(6)} %copy.9.live_hbm, bf16[24,128,128]{2,1,0:T(8,128)(2,1)} %bitcast.2, s32[4,1]{1,0:T(4,128)} %copy.7.mask_hbm), custom_call_target="tpu_custom_call" | custom-call | flops 1073741824 | bytes 2097152 | tf_op jit(solution)/shard_map/pallas_call | solution.py:529
  100.7 1.6 %copy.10 = bf16[512,128]{1,0:T(8,128)(2,1)} copy(bf16[512,128]{1,0:T(8,128)(2,1)} %shard_map.64) | data formatting | bytes 262144
Async XLA Ops:
  0.7 0.7 copy-start

commit v4 on v3

--- a/solution.py
+++ b/solution.py
@@ -335,13 +335,6 @@
         for q in range(2):
             bbuf[n, y, q] = b_ref[chosen(r - zl + g, q)]
 
-    def sent_b(n):
-        def one(d, _):
-            b_copy(n, d).wait_send()
-            return 0
-
-        lax.fori_loop(1, NY, one, 0)
-
     def r_copy(d, i):
         src = ix2.at[i, pl.ds(rem(y + d, NY) * NZ, NZ)]
         return remote(src, rbuf.at[y, i], s_r.at[d, i], r_r.at[d, i], at_y(d))
@@ -364,6 +357,7 @@
     send_r()
     send_b(1)
     send_b(2)
+    send_b(3)
 
     def rows_arrive():
         def wait_r(d, _):
@@ -450,14 +444,12 @@
     send_s2(3)
     send_x(3, 0)
     near_chunks(0)
-    rows_arrive()
     own_chunk(2)
     far_chunk(0)
     near_chunks(1)
-    sent_b(0)
-    send_b(3)
     own_chunk(3)
     far_chunk(1)
+    rows_arrive()
     hand_over(0)
     near_chunks(2)
     hand_over(1)
@@ -500,7 +492,7 @@
         lax.fori_loop(1, N_COL, sent, 0)
 
     def sent_y(d, _):
-        for n in range(1, 4):
+        for n in range(4):
             b_copy(n, d).wait_send()
         r_copy(d, 0).wait_send()
         pl.when(two)(lambda: r_copy(d, 1).wait_send())

time: 102 us -> 107 us (1.049); the launches traced: 102 us -> 106 us
  Pallas kernels: 98.7 us -> 102 us
    pallas_call x1, Pallas kernels: 98.7 us -> 102 us  [per_device(): pl.pallas_call(kernel, out_shape=jax.ShapeDtypeStruct((RCAP * BS, BS), bf...]
where the time goes in v4:
time: 107 us; the launch traced here: 106 us
  Pallas kernels  102 us (95%)
  local copies, waits for them, and re-layouts  2.88 us (3%)
    pallas_call x1, Pallas kernels, per_device(): pl.pallas_call(kernel, out_shape=jax.ShapeDtypeStruct((RCAP * BS, BS), bf...  102 us
    unnamed x4, local copies, waits for them, and re-layouts  2.88 us

profile of v4, /device:TPU:1, one launch (start us, length us, event | category | flops | bytes accessed | tf_op | source)
XLA Modules:
  0.0 105.8 jit_solution(6746777680429061624)
XLA Ops:
  0.7 0.0 copy-start
  0.7 0.6 copy-done
  1.3 0.7 copy.7.mask_hbm
  2.0 102.2 %shard_map.64 = bf16[512,128]{1,0:T(8,128)(2,1)} custom-call(bf16[11,128,128]{2,1,0:T(8,128)(2,1)} %bitcast.3, s32[1,11]{1,0:T(1,128)} %row_hbm.1, s32[1,11]{1,0:T(1,128)} %col_hbm.1, s32[1]{0:T(128)S(6)} %copy.9.live_hbm, bf16[24,128,128]{2,1,0:T(8,128)(2,1)} %bitcast.2, s32[4,1]{1,0:T(4,128)} %copy.7.mask_hbm), custom_call_target="tpu_custom_call" | custom-call | flops 1073741824 | bytes 2097152 | tf_op jit(solution)/shard_map/pallas_call | solution.py:521
  104.2 1.6 %copy.10 = bf16[512,128]{1,0:T(8,128)(2,1)} copy(bf16[512,128]{1,0:T(8,128)(2,1)} %shard_map.64) | data formatting | bytes 262144
Async XLA Ops:
  0.7 0.7 copy-start
